TPU v7x, 512 devices: a whole 4x4x16 slice. The times are simulated.
512 devices in a mesh: grp: 16 (over y_lo, x, core), fsdp: 32 (over z, y_hi).
Axes of the slice: x: 4, y: 4 (y_hi: 2, y_lo: 2; y = y_hi * 2 + y_lo), z: 16, core: 2. Of those that a mesh axis runs over, the one named last changes fastest.
Arguments:
- raw_clips: bfloat16 [16, 1024, 8, 2048], P('grp', 'fsdp'), may hold values from -6 to 6
- clip_lengths: int32 [16, 32, 32], P('grp', 'fsdp'), may hold values from 1 to 8, 160 in all within a row
- clip_routes: int32 [16, 1024, 1], P('grp', 'fsdp'), may hold values from 0 to 31; in each aligned block of 32 rows (0 to 31, 32 to 63, ..., all dimensions but the last counted through in order) at most 2 rows name the same one
- w_spectral: bfloat16 [1024, 4096], P('fsdp', 'grp'), may hold values from -0.1875 to 0.1875
- norm_gain: float32 [4096], replicated, may hold values from 0.25 to 1.75
- room_heads: bfloat16 [32, 4096, 256], P('fsdp'), may hold values from -0.09375 to 0.09375
Outputs:
- decay_curves: bfloat16 [16, 1024, 8, 256], P('grp', 'fsdp')
Inputs may be any that keep to these rules, and one draw needn't show every extreme that they name: `clip_routes`: among the 32 clips of one device, no room head is named more than 2 times, and in every draw some device names some room head exactly 2 times; every room head is named by some clip. `clip_lengths`: the 32 lengths of one device sum to 160, and the longest of them is exactly 8.
All inputs are finite; a program needn't handle non-finite values.
Results may differ from a plain program's by a relative error of at most 0.007.
Values may be sent and summed in bfloat16 or wider, within the bound.
A program may use at most 64 MiB of HBM per device.

v0:
```python
import math

import jax
import jax.numpy as jnp
from jax import lax
from jax.sharding import PartitionSpec as P

SLOTS = 2


norm_epsilon = 1e-05


def spectral_table(window):
    sample_idx = jnp.arange(window, dtype=jnp.int32)
    bin_idx = jnp.arange(window // 2, dtype=jnp.int32)
    products = sample_idx[:, None] * bin_idx[None, :] % window
    angles = products.astype(jnp.float32) * (2.0 * math.pi / window)
    taper_window = 0.5 - 0.5 * jnp.cos(sample_idx.astype(jnp.float32) * (2.0 * math.pi / window))
    cosines = taper_window[:, None] * jnp.cos(angles)
    sines = -taper_window[:, None] * jnp.sin(angles)
    return jnp.concatenate([cosines, sines], axis=1).astype(jnp.bfloat16)


def log_energy(frames, dft_table):
    window = frames.shape[1]
    bin_count = window // 2
    spectra = jnp.dot(frames, dft_table, preferred_element_type=jnp.float32)
    real_part = spectra[:, :bin_count]
    imag_part = spectra[:, bin_count:]
    return jnp.log1p((real_part * real_part + imag_part * imag_part) / window)


def rms_normed(projected, norm_gain):
    mean_square = jnp.mean(projected * projected, axis=-1, keepdims=True)
    return (projected * lax.rsqrt(mean_square + norm_epsilon) * norm_gain).astype(jnp.bfloat16)


def make_adder(rows, weight_piece):
    return jnp.dot(rows, weight_piece, preferred_element_type=jnp.float32)


def project_whole(rows, w_spectral, norm_gain):
    columns = lax.all_gather(w_spectral, "grp", axis=1, tiled=True)
    projected = make_adder(rows, lax.all_gather(columns, "fsdp", axis=0, tiled=True))
    return rms_normed(projected, norm_gain)


def body(raw_clips, clip_lengths, clip_routes, w_spectral, norm_gain, room_heads):
    clip_count = raw_clips.shape[1]
    frame_slots = raw_clips.shape[2]
    window = raw_clips.shape[3]
    bin_count = window // 2
    shards = lax.axis_size("fsdp")
    dft_table = spectral_table(window)
    features = log_energy(raw_clips.reshape(-1, window), dft_table).reshape(
        clip_count, frame_slots, bin_count
    )
    lengths_now = clip_lengths.reshape(clip_count)
    alive_mask = (jnp.arange(frame_slots, dtype=jnp.int32)[None, :] < lengths_now[:, None]).astype(
        jnp.float32
    )
    clip_mean = jnp.sum(features * alive_mask[:, :, None], axis=1) / lengths_now[:, None].astype(
        jnp.float32
    )
    centered = (features - clip_mean[:, None, :]).astype(jnp.bfloat16)
    target = clip_routes.reshape(clip_count)
    clip_idx = jnp.arange(clip_count, dtype=jnp.int32)
    earlier = clip_idx[:, None] > clip_idx[None, :]
    same_target = jnp.logical_and(target[:, None] == target[None, :], earlier)
    slot_rank = jnp.sum(same_target.astype(jnp.int32), axis=1)
    slot_index = target * SLOTS + slot_rank
    placing = (jnp.arange(shards * SLOTS, dtype=jnp.int32)[:, None] == slot_index[None, :]).astype(
        jnp.bfloat16
    )
    width = centered.shape[2]
    spread = jnp.dot(placing, centered.reshape(clip_count, -1), preferred_element_type=jnp.float32)
    received = lax.all_to_all(
        spread.astype(jnp.bfloat16).reshape(shards, SLOTS, frame_slots, width),
        "fsdp",
        split_axis=0,
        concat_axis=0,
        tiled=True,
    )
    hidden = project_whole(received.reshape(-1, bin_count), w_spectral, norm_gain)
    curves = jnp.dot(hidden, room_heads[0], preferred_element_type=jnp.float32).astype(jnp.bfloat16)
    curves = curves.reshape(shards, SLOTS, frame_slots, -1)
    returned = lax.all_to_all(curves, "fsdp", split_axis=0, concat_axis=0, tiled=True)
    gathered = jnp.dot(
        placing.T, returned.reshape(shards * SLOTS, -1), preferred_element_type=jnp.float32
    )
    gathered = gathered.astype(jnp.bfloat16).reshape(clip_count, frame_slots, -1)
    return (gathered * alive_mask[:, :, None].astype(jnp.bfloat16))[None]


def solution(mesh):
    return jax.shard_map(
        body,
        mesh=mesh,
        in_specs=(
            P("grp", "fsdp", None, None),
            P("grp", "fsdp", None),
            P("grp", "fsdp", None),
            P("fsdp", "grp"),
            P(),
            P("fsdp", None, None),
        ),
        out_specs=P("grp", "fsdp", None, None),
        check_vma=False,
    )
```

profile of v0, /device:TPU:24, one launch (start us, length us, event | category | flops | bytes accessed | tf_op | source)
XLA Modules:
  0.0 286.4 jit_solution(163988528811162332)
XLA Ops:
  6.5 0.0 copy-start
  6.5 0.0 copy-start.3
  6.5 0.0 all-gather.2.cloned.1.call-start
  6.5 21.3 %all_gather.6 = bf16[32,4096]{1,0:T(8,128)(2,1)} all-gather(bf16[32,256]{1,0:T(8,128)(2,1)} %param.9), channel_id=1, replica_groups=mesh['grp'=16,'fsdp'=32] {'grp'}, dimensions={1}, use_global_device_ids=true | all-gather | bytes 278528 | tf_op jit(solution)/shard_map/all_gather | solution.py:44
  27.9 0.0 all-gather.2.cloned.1.call-update
  27.9 0.1 fusion.30
  27.9 0.1 multiply_subtract_fusion
  28.0 0.7 fusion.29
  28.7 34.7 %multiply_convert_fusion.1 = (bf16[2048,1024]{1,0:T(8,128)(2,1)S(1)}, bf16[2048,1024]{1,0:T(8,128)(2,1)S(1)}) fusion(f32[2048]{0:T(1024)S(1)} %fusion.30, f32[2048]{0:T(1024)S(1)} %multiply_subtract_fusion), kind=kLoop, calls=%fused_computation.13 | loop fusion | flops 37748736 | bytes 8404992 | tf_op jit(solution)/shard_map/convert.1
  63.4 0.0 copy-done.3
  63.4 0.0 copy-start.2
  63.4 2.3 fusion.13
  65.8 0.0 copy-start.4
  65.8 0.7 fusion.23
  66.6 1.3 reshape.141
  67.8 0.0 copy-done.2
  67.8 0.1 broadcast_divide_fusion
  67.9 0.1 sub.24
  68.0 0.6 copy.7
  68.7 0.0 copy-done.4
  68.7 0.2 convert_reduce_fusion
  68.9 1.7 convolution_convert_fusion
  70.5 0.6 copy.8
  71.2 71.3 %all_to_all.10 = bf16[32,2,8,1024]{3,2,1,0:T(8,128)(2,1)S(1)} all-to-all(bf16[32,2,8,1024]{3,2,1,0:T(8,128)(2,1)S(1)} %bitcast.39), channel_id=1, replica_groups=mesh['grp'=16,'fsdp'=32] {'fsdp'}, dimensions={0} | all-to-all | bytes 2097152 | tf_op jit(solution)/shard_map/all_to_all | solution.py:78
  142.4 100.0 %all-gather.2.cloned.1.call-done = bf16[1024,4096]{1,0:T(8,128)(2,1)} async-done(((bf16[32,4096]{1,0:T(8,128)(2,1)}), bf16[1024,4096]{1,0:T(8,128)(2,1)}) %all-gather.2.cloned.1.call-update) | async-done | bytes 8388624 | tf_op jit(solution)/shard_map/all_gather | solution.py:45
  242.5 0.0 copy-start.1
  242.5 7.1 %multiply_reduce_fusion = (f32[512]{0:T(512)S(1)}, f32[512,4096]{1,0:T(8,128)S(1)}) fusion(bf16[512,1024]{1,0:T(8,128)(2,1)S(1)} %bitcast.41, bf16[1024,4096]{1,0:T(8,128)(2,1)} %all-gather.2.cloned.1.call-done), kind=kOutput, calls=%fused_computation.12 | convolution fusion | flops 4299161088 | bytes 17827840 | tf_op jit(solution)/shard_map/dot_general | solution.py:40
  249.6 0.0 copy-done
  249.6 0.0 copy-done.1
  249.6 1.4 fusion.17
  251.0 27.5 %all_to_all.11 = bf16[32,2,8,256]{3,2,1,0:T(8,128)(2,1)S(1)} all-to-all(bf16[32,2,8,256]{3,2,1,0:T(8,128)(2,1)S(1)} %bitcast.40), channel_id=1, replica_groups=mesh['grp'=16,'fsdp'=32] {'fsdp'}, dimensions={0} | all-to-all | bytes 524288 | tf_op jit(solution)/shard_map/all_to_all | solution.py:88
  278.5 0.1 copy.9
  278.5 0.2 convolution_convert_fusion.1
  278.8 0.8 bitcast_multiply_fusion.1
  (4 shorter events, 0.0 us)
Async XLA Ops:
  6.5 243.1 %copy-start = (bf16[1,4096,256]{2,1,0:T(8,128)(2,1)S(1)}, bf16[1,4096,256]{2,1,0:T(8,128)(2,1)}, u32[]{:S(2)}) copy-start(bf16[1,4096,256]{2,1,0:T(8,128)(2,1)} %param.11) | copy-start | bytes 6291460
  6.5 56.9 %copy-start.3 = (bf16[1,32,8,2048]{3,2,1,0:T(8,128)(2,1)S(1)}, bf16[1,32,8,2048]{3,2,1,0:T(8,128)(2,1)}, u32[]{:S(2)}) copy-start(bf16[1,32,8,2048]{3,2,1,0:T(8,128)(2,1)} %param.6) | copy-start | bytes 3145732
  6.5 235.9 %all-gather.2.cloned.1.call-start = ((), (), s32[]{:S(2)}) async-start(), calls=%async_computation.2 | async-start | bytes 8650752 | tf_op jit(solution)/shard_map/all_gather | solution.py:45
  63.4 4.4 %copy-start.2 = (s32[1,1,32]{2,1,0:T(1,128)S(1)}, s32[1,1,32]{2,1,0:T(1,128)}, u32[]{:S(2)}) copy-start(s32[1,1,32]{2,1,0:T(1,128)} %param.7) | copy-start | bytes 388
  65.8 2.9 copy-start.4
  242.5 7.2 %copy-start.1 = (f32[4096]{0:T(1024)S(1)}, f32[4096]{0:T(1024)}, u32[]{:S(2)}) copy-start(f32[4096]{0:T(1024)} %param.10) | copy-start | bytes 49156
Sparse Core Ops, SparseCore 0:
  28.0 214.4 all-gather.1
where the time goes:
time: 287 us; the launch traced here: 286 us
  blocking collectives  120 us (42%)
  waiting for transfers between devices  100 us (35%)
  other arithmetic  37.3 us (13%)
  between operations  13.5 us (5%)
  matrix products  12.7 us (4%)
    all_gather x1, waiting for transfers between devices, project_whole(): lax.all_gather(columns, 'fsdp', axis=0, tiled=True)  100 us
    all_to_all x1, blocking collectives, body(): lax.all_to_all(spread.astype(jnp.bfloat16).reshape(shards, SLOTS, frame_s...  71.3 us
    another operation x1, other arithmetic  34.7 us
    all_to_all x1, blocking collectives, body(): lax.all_to_all(curves, 'fsdp', split_axis=0, concat_axis=0, tiled=True)  27.5 us
    all_gather x1, blocking collectives, project_whole(): columns = lax.all_gather(w_spectral, 'grp', axis=1, tiled=True)  21.3 us
    dot_general x1, matrix products, make_adder(): return jnp.dot(rows, weight_piece, preferred_element_type=jnp.float32)  7.12 us
  transfers between devices with their start and end apart: 1, of which 1 were waited for; matrix products, arithmetic and copies ran while one was open for 15% of the time, Pallas kernels for 0%

commit v1 on v0

v1 whole, which is shorter than its diff:
```python
import functools
import math

import jax
import jax.numpy as jnp
from jax import lax
from jax.experimental import pallas as pl
from jax.experimental.pallas import tpu as pltpu
from jax.sharding import PartitionSpec as P

SLOTS = 2
MESH = pl.DeviceIdType.MESH
norm_epsilon = 1e-05


def remote(src, dst, send_sem, recv_sem, device):
    return pltpu.make_async_remote_copy(
        src_ref=src,
        dst_ref=dst,
        send_sem=send_sem,
        recv_sem=recv_sem,
        device_id=device,
        device_id_type=MESH,
    )


def loop(low, high, step):
    def body(i, carry):
        step(i)
        return carry

    lax.fori_loop(low, high, body, 0)


def kernel(
    n,
    raw_ref, w_ref, gain_ref, head_ref, srow_ref, scol_ref, live_ref,
    out_ref,
    tab, trc, trs, c_own, c_pair, cs, cr, wz, wr, ws, mc, mz, mr, gp, gz, gs, gf, y, yr, ms_send, ms_recv,
    w1s, w1r, wss, wsr, w2s, w2r, m1s, m1r, m2s, m2r, g1s, g1r, g2s, g2r, c1s, c1r, c3s, c3r, xs, xr,
):
    rooms = 2 * n
    rows, window = raw_ref.shape
    bins = c_own.shape[1]
    half = bins // 2
    rb = w_ref.shape[0]
    g, f = lax.axis_index("grp"), lax.axis_index("fsdp")
    z, h = f // 2, lax.rem(f, 2)
    core = lax.rem(g, 2)
    me = 2 * g + h
    pair = (g + 1 - 2 * core, f)

    def in_plane(q):
        return (q // 2, 2 * z + lax.rem(q, 2))

    def in_column(q):
        return (g, 2 * q + h)

    barrier = pltpu.get_barrier_semaphore()

    def greet_plane(d):
        pl.semaphore_signal(barrier, inc=1, device_id=in_plane(lax.rem(me + d, rooms)), device_id_type=MESH)

    def greet_column(d):
        pl.semaphore_signal(barrier, inc=1, device_id=in_column(lax.rem(z + d, n)), device_id_type=MESH)

    loop(1, rooms, greet_plane)
    loop(1, n, greet_column)
    pl.semaphore_wait(barrier, rooms - 1 + n - 1)

    def w1_copy(q):
        return remote(w_ref, wz.at[z], w1s.at[q], w1r.at[z], in_column(q))

    def w1_arrival(q):
        return remote(w_ref, wz.at[q], w1s.at[q], w1r.at[q], in_column(q))

    def ws_copy(q):
        return remote(w_ref, ws.at[g], wss.at[q], wsr.at[g], (q, f))

    def ws_arrival(q):
        return remote(w_ref, ws.at[q], wss.at[q], wsr.at[q], (q, f))

    loop(1, n, lambda d: w1_copy(lax.rem(z + d, n)).start())
    loop(1, n, lambda d: ws_copy(lax.rem(g + d, n)).start())
    wz[z] = w_ref[...]
    ws[g] = w_ref[...]

    wide = bins + 128
    coarse = window // 64
    lane = lax.broadcasted_iota(jnp.int32, (8, wide), 1)
    bin_idx = jnp.where(
        lane < bins, 2 * rb * ((lane % half) // rb) + rb * (lane // half) + lane % rb, 1
    )
    sub = lax.broadcasted_iota(jnp.int32, (8, wide), 0)

    def trig_rows(base, factor, first):
        angle = (((sub + first) * factor * bin_idx) & (window - 1)).astype(jnp.float32) * (
            2.0 * math.pi / window
        )
        trc[pl.ds(base, 8), :] = jnp.cos(angle)
        trs[pl.ds(base, 8), :] = jnp.sin(angle)

    loop(0, coarse // 8, lambda i: trig_rows(pl.multiple_of(8 * i, 8), 64, 8 * i))
    trig_rows(coarse, 8, 0)
    trig_rows(coarse + 8, 1, 0)

    def table_rows(a):
        ac, as_ = trc[pl.ds(a, 1), :], trs[pl.ds(a, 1), :]
        bc, bs = trc[coarse : coarse + 8, :], trs[coarse : coarse + 8, :]
        cc, cs_ = trc[coarse + 8 : coarse + 16, :], trs[coarse + 8 : coarse + 16, :]
        mid_c = ac * bc - as_ * bs
        mid_s = as_ * bc + ac * bs
        for b in range(0, 8, 2):
            real, imag = [], []
            for e in (b, b + 1):
                c1, s1 = mid_c[e : e + 1, :], mid_s[e : e + 1, :]
                cosines = c1 * cc - s1 * cs_
                sines = s1[:, :bins] * cc[:, :bins] + c1[:, :bins] * cs_[:, :bins]
                taper = 0.5 - 0.5 * cosines[:, bins:]
                taper = jnp.concatenate([taper] * (bins // 128), axis=1)
                real.append(taper * cosines[:, :bins])
                imag.append(-(taper * sines))
            here = pl.ds(pl.multiple_of(64 * a + 8 * b, 16), 16)
            tab[here, :bins] = jnp.concatenate(real, axis=0).astype(jnp.bfloat16)
            tab[here, bins:] = jnp.concatenate(imag, axis=0).astype(jnp.bfloat16)

    loop(0, coarse, table_rows)

    block = min(256, bins)

    def spectra_block(i):
        here = pl.ds(pl.multiple_of(i * block, block), block)
        there = pl.ds(pl.multiple_of(bins + i * block, block), block)
        frames = raw_ref[...]
        re = jnp.dot(frames, tab[:, here], preferred_element_type=jnp.float32)
        im = jnp.dot(frames, tab[:, there], preferred_element_type=jnp.float32)
        energy = jnp.log1p((re * re + im * im) / window)
        kept = (energy * live_ref[...]).reshape(rows // 8, 8, block)
        mean = jnp.sum(kept, axis=1, keepdims=True)
        centered = energy.reshape(rows // 8, 8, block) - mean
        c_own[:, here] = centered.reshape(rows, block).astype(jnp.bfloat16)

    loop(0, bins // block, spectra_block)

    pair_copy = remote(c_own, c_pair, xs.at[0], xr.at[0], pair)
    pair_copy.start()

    def w2_copy(src, q):
        return remote(wz.at[src], wr.at[g, h], w2s.at[q], w2r.at[me], in_plane(q))

    def w2_arrival(q):
        return remote(wz.at[0], wr.at[q // 2, lax.rem(q, 2)], w2s.at[q], w2r.at[q], in_plane(q))

    def w2_send(src):
        for side in range(2):
            q = 2 * src + side

            @pl.when(q != me)
            def _():
                w2_copy(src, q).start()

    def w2_forward(d):
        src = lax.rem(z + d, n)
        w1_arrival(src).wait_recv()
        w2_send(src)

    w2_send(z)
    loop(1, n, w2_forward)
    wr[g, h] = wz[g]

    width = cs.shape[1]
    place = (
        lax.broadcasted_iota(jnp.int32, (rooms * width, rows), 0) == srow_ref[...]
    ).astype(jnp.bfloat16)

    def place_block(i):
        here = pl.ds(pl.multiple_of(i * block, block), block)
        spread = jnp.dot(place, c_own[:, here], preferred_element_type=jnp.float32)
        cs[:, :, here] = spread.astype(jnp.bfloat16).reshape(rooms, width, block)

    loop(0, bins // block, place_block)

    def c1_copy(q):
        return remote(cs.at[q], cr.at[me], c1s.at[q], c1r.at[me], in_plane(q))

    def c1_arrival(q):
        return remote(cs.at[q], cr.at[q], c1s.at[q], c1r.at[q], in_plane(q))

    loop(1, rooms, lambda d: c1_copy(lax.rem(me + d, rooms)).start())
    cr[me] = cs[me]

    loop(1, rooms, lambda d: w2_arrival(lax.rem(me + d, rooms)).wait_recv())
    loop(1, n, lambda d: ws_arrival(lax.rem(g + d, n)).wait_recv())

    w_rows = jnp.concatenate([wr[k].reshape(2 * rb, -1) for k in range(n)], axis=1)
    w_cols = jnp.concatenate([ws[k] for k in range(n)], axis=1)
    gram = lax.dot_general(
        w_rows,
        jnp.concatenate([w_cols] * 4, axis=0),
        (((1,), (1,)), ((), ())),
        preferred_element_type=jnp.float32,
    )
    quarter = lax.broadcasted_iota(jnp.int32, (16, 128), 1) // rb
    piece = jnp.zeros((16, 128), jnp.float32)
    for q in range(4):
        piece = jnp.where(quarter == q, gram[16 * q : 16 * q + 16, :], piece)
    gp[...] = piece.astype(jnp.bfloat16)

    def g1_copy(q):
        return remote(gp, gz.at[z], g1s.at[q], g1r.at[z], in_column(q))

    def g1_arrival(q):
        return remote(gp, gz.at[q], g1s.at[q], g1r.at[q], in_column(q))

    loop(1, n, lambda d: g1_copy(lax.rem(z + d, n)).start())
    gz[z] = gp[...]

    scaled = (w_rows.astype(jnp.float32) * gain_ref[...]).astype(jnp.bfloat16)
    mc[...] = jnp.dot(scaled, head_ref[...], preferred_element_type=jnp.float32).astype(jnp.bfloat16)

    def m1_copy(q):
        return remote(mc, mz.at[z], m1s.at[q], m1r.at[z], in_column(q))

    def m1_arrival(q):
        return remote(mc, mz.at[q], m1s.at[q], m1r.at[q], in_column(q))

    loop(1, n, lambda d: m1_copy(lax.rem(z + d, n)).start())
    mz[z] = mc[...]

    loop(1, n, lambda d: g1_arrival(lax.rem(z + d, n)).wait_recv())
    for tile in range(n // 4):
        pieces = [gz[4 * tile + k].astype(jnp.float32) for k in range(4)]
        for q in range(4):
            strip = jnp.zeros((16, 128), jnp.float32)
            for k in range(4):
                shift = (rb * (k - q)) % 128
                moved = pltpu.roll(pieces[k], shift, 1) if shift else pieces[k]
                strip = jnp.where(quarter == k, moved, strip)
            gs[16 * q : 16 * q + 16, 128 * tile : 128 * tile + 128] = strip.astype(jnp.bfloat16)

    def g2_copy(q):
        return remote(gs, gf.at[g], g2s.at[q], g2r.at[g], (2 * (q // 2) + h, 2 * z + lax.rem(q, 2)))

    def g2_arrival(k):
        return remote(gs, gf.at[k], g2s.at[0], g2r.at[k], (k, 2 * z + core))

    own = 2 * (g // 2) + h

    def g2_each(act):
        def step(d):
            q = lax.rem(own + d, n)

            @pl.when((2 * (q // 2) + h != g) | (lax.rem(q, 2) != h))
            def _():
                act(g2_copy(q))

        return step

    loop(0, n, g2_each(lambda copy: copy.start()))

    @pl.when(h == core)
    def _():
        gf[g] = gs[...]

    def m2_copy(q):
        return remote(mz.at[q], mr.at[g], m2s.at[q], m2r.at[g], (q, f))

    def m2_arrival(q):
        return remote(mz.at[q], mr.at[q], m2s.at[q], m2r.at[q], (q, f))

    def m2_send(src):
        @pl.when(src != g)
        def _():
            m2_copy(src).start()

    def m2_forward(d):
        src = lax.rem(z + d, n)
        m1_arrival(src).wait_recv()
        m2_send(src)

    m2_send(z)
    loop(1, n, m2_forward)
    mr[g] = mz[g]

    pair_copy.wait_recv()

    def g2_wait(k):
        @pl.when((k != g) | (h != core))
        def _():
            g2_arrival(k).wait_recv()

    loop(0, n, g2_wait)
    mine = pl.ds(pl.multiple_of(core * half, half), half)
    gram_low = gf[:, :rb, :].reshape(half, half)
    gram_high = gf[:, rb:, :].reshape(half, half)

    def squares(frames):
        out = jnp.dot(frames[:, :half], gram_low, preferred_element_type=jnp.float32)
        out = out + jnp.dot(frames[:, half:], gram_high, preferred_element_type=jnp.float32)
        return jnp.sum(out * frames[:, mine].astype(jnp.float32), axis=1, keepdims=True)

    ms_send[...] = jnp.broadcast_to(squares(c_pair), ms_send.shape)
    ms_copy = remote(ms_send, ms_recv, xs.at[1], xr.at[1], pair)
    ms_copy.start()
    squares_here = squares(c_own)

    loop(1, rooms, lambda d: c1_arrival(lax.rem(me + d, rooms)).wait_recv())
    loop(1, n, lambda d: m2_arrival(lax.rem(g + d, n)).wait_recv())
    low = mr[:, :rb, :].reshape(half, -1)
    high = mr[:, rb:, :].reshape(half, -1)
    got = cr[...].reshape(rooms * width, bins)
    curves = jnp.dot(got[:, :half], low, preferred_element_type=jnp.float32)
    curves = curves + jnp.dot(got[:, half:], high, preferred_element_type=jnp.float32)
    y[...] = curves.astype(jnp.bfloat16).reshape(y.shape)

    def c3_copy(q):
        return remote(y.at[q], yr.at[me], c3s.at[q], c3r.at[me], in_plane(q))

    def c3_arrival(q):
        return remote(y.at[q], yr.at[q], c3s.at[q], c3r.at[q], in_plane(q))

    loop(1, rooms, lambda d: c3_copy(lax.rem(me + d, rooms)).start())
    yr[me] = y[me]

    loop(1, n, lambda d: w1_copy(lax.rem(z + d, n)).wait_send())
    loop(1, n, lambda d: ws_copy(lax.rem(g + d, n)).wait_send())
    loop(1, n, lambda d: g1_copy(lax.rem(z + d, n)).wait_send())
    loop(1, n, lambda d: m1_copy(lax.rem(z + d, n)).wait_send())
    loop(1, n, lambda d: m2_copy(lax.rem(g + d, n)).wait_send())
    loop(1, rooms, lambda d: w2_copy(0, lax.rem(me + d, rooms)).wait_send())
    loop(1, rooms, lambda d: c1_copy(lax.rem(me + d, rooms)).wait_send())
    loop(0, n, g2_each(lambda copy: copy.wait_send()))
    pair_copy.wait_send()

    ms_copy.wait()
    total = squares_here + ms_recv[:, :1]
    mean_square = jnp.maximum(total, 0.0) / head_ref.shape[0]
    scale = lax.rsqrt(mean_square + norm_epsilon)
    take = (
        lax.broadcasted_iota(jnp.int32, (rows, rooms * width), 1) == scol_ref[...]
    ).astype(jnp.bfloat16)
    loop(1, rooms, lambda d: c3_arrival(lax.rem(me + d, rooms)).wait_recv())
    back = jnp.dot(take, yr[...].reshape(rooms * width, -1), preferred_element_type=jnp.float32)
    out_ref[...] = (back * scale).astype(jnp.bfloat16)
    loop(1, rooms, lambda d: c3_copy(lax.rem(me + d, rooms)).wait_send())


def body(raw_clips, clip_lengths, clip_routes, w_spectral, norm_gain, room_heads):
    _, clip_count, slots, window = raw_clips.shape
    n = lax.axis_size("grp")
    rooms = lax.axis_size("fsdp")
    rows = clip_count * slots
    bins = window // 2
    rb, kc = w_spectral.shape
    curve = room_heads.shape[2]
    width = SLOTS * slots

    lengths = clip_lengths.reshape(clip_count)
    target = clip_routes.reshape(clip_count)
    clip_idx = jnp.arange(clip_count, dtype=jnp.int32)
    frame_idx = jnp.arange(slots, dtype=jnp.int32)
    same = (target[:, None] == target[None, :]) & (clip_idx[:, None] > clip_idx[None, :])
    slot = target * SLOTS + jnp.sum(same.astype(jnp.int32), axis=1)
    live = frame_idx[None, :] < lengths[:, None]
    slot_rows = jnp.where(live, slot[:, None] * slots + frame_idx[None, :], -1)
    weights = live.astype(jnp.float32) / lengths[:, None].astype(jnp.float32)

    bf16, f32 = jnp.bfloat16, jnp.float32
    vmem, sems = pltpu.VMEM, lambda k: pltpu.SemaphoreType.DMA((k,))
    coarse = window // 64
    out = pl.pallas_call(
        functools.partial(kernel, n),
        out_shape=jax.ShapeDtypeStruct((rows, curve), bf16),
        in_specs=[pl.BlockSpec(memory_space=pltpu.VMEM)] * 7,
        out_specs=pl.BlockSpec(memory_space=pltpu.VMEM),
        scratch_shapes=[
            vmem((window, 2 * bins), bf16),
            vmem((coarse + 16, bins + 128), f32),
            vmem((coarse + 16, bins + 128), f32),
            vmem((rows, bins), bf16),
            vmem((rows, bins), bf16),
            vmem((rooms, width, bins), bf16),
            vmem((rooms, width, bins), bf16),
            vmem((n, rb, kc), bf16),
            vmem((n, 2, rb, kc), bf16),
            vmem((n, rb, kc), bf16),
            vmem((2 * rb, curve), bf16),
            vmem((n, 2 * rb, curve), bf16),
            vmem((n, 2 * rb, curve), bf16),
            vmem((16, 128), bf16),
            vmem((n, 16, 128), bf16),
            vmem((2 * rb, bins // 2), bf16),
            vmem((n, 2 * rb, bins // 2), bf16),
            vmem((rooms, width, curve), bf16),
            vmem((rooms, width, curve), bf16),
            vmem((rows, 128), f32),
            vmem((rows, 128), f32),
            sems(n), sems(n), sems(n), sems(n),
            sems(rooms), sems(rooms),
            sems(n), sems(n), sems(n), sems(n),
            sems(n), sems(n), sems(n), sems(n),
            sems(rooms), sems(rooms), sems(rooms), sems(rooms),
            sems(2), sems(2),
        ],
        compiler_params=pltpu.CompilerParams(
            collective_id=0, has_side_effects=True, vmem_limit_bytes=56 * 2**20
        ),
    )(
        raw_clips.reshape(rows, window),
        w_spectral,
        norm_gain.reshape(1, -1),
        room_heads[0],
        slot_rows.reshape(1, rows),
        slot_rows.reshape(rows, 1),
        weights.reshape(rows, 1),
    )
    return out.reshape(1, clip_count, slots, curve)


def solution(mesh):
    return jax.shard_map(
        body,
        mesh=mesh,
        in_specs=(
            P("grp", "fsdp", None, None),
            P("grp", "fsdp", None),
            P("grp", "fsdp", None),
            P("fsdp", "grp"),
            P(),
            P("fsdp", None, None),
        ),
        out_specs=P("grp", "fsdp", None, None),
        check_vma=False,
    )
```

time: 287 us -> 103 us (0.36)
  the two profiles are of different devices: /device:TPU:24 before, /device:TPU:1 now
where the time goes in v1:
time: 103 us; the launch traced here: 102 us
  Pallas kernels  94.8 us (92%)
  local copies, waits for them, and re-layouts  3.72 us (4%)
  other arithmetic  3.69 us (4%)
    pallas_call x1, Pallas kernels, body(): pl.pallas_call(functools.partial(kernel, n), out_shape=jax.ShapeDtypeStru...  94.8 us

profile of v1, /device:TPU:1, one launch (start us, length us, event | category | flops | bytes accessed | tf_op | source)
XLA Modules:
  0.0 102.2 jit_solution(14033407688931840013)
XLA Ops:
  0.0 0.9 convert_reduce_fusion
  0.9 0.7 add_multiply_fusion
  1.6 0.7 bitcast_convert_fusion
  2.2 0.7 add_select_fusion
  3.0 0.7 select_n.25.srow_ref
  3.6 0.7 convert_divide_fusion
  4.4 0.7 div.21.live_ref
  5.1 0.8 select_n.27.scol_ref
  5.8 94.8 %shard_map.64 = bf16[256,256]{1,0:T(8,128)(2,1)} custom-call(bf16[256,2048]{1,0:T(8,128)(2,1)} %bitcast.9, bf16[32,256]{1,0:T(8,128)(2,1)} %w_ref.1, f32[1,4096]{1,0:T(1,128)} %bitcast.11, bf16[4096,256]{1,0:T(8,128)(2,1)} %bitcast.8, s32[1,256]{1,0:T(1,128)} %select_n.25.srow_ref, s32[256,1]{1,0:T(8,128)} %select_n.27.scol_ref, f32[256,1]{1,0:T(8,128)} %div.21.live_ref), custom_call_target="tpu_custom_call" | custom-call | tf_op jit(solution)/shard_map/pallas_call | solution.py:371
  100.7 1.6 %copy.12 = bf16[1,32,8,256]{3,2,1,0:T(8,128)(2,1)} copy(bf16[1,32,8,256]{3,2,1,0:T(8,128)(2,1)} %bitcast.10) | data formatting | bytes 262144

commit v2 on v1

--- a/solution.py
+++ b/solution.py
@@ -34,9 +34,10 @@
 
 def kernel(
     n,
-    raw_ref, w_ref, gain_ref, head_ref, srow_ref, scol_ref, live_ref,
+    raw_ref, w_ref, gain_ref, head_ref, len_ref, route_ref,
     out_ref,
-    tab, trc, trs, c_own, c_pair, cs, cr, wz, wr, ws, mc, mz, mr, gp, gz, gs, gf, y, yr, ms_send, ms_recv,
+    tab, trc, trs, slot_col, slot_row, weight, c_own, c_pair, cs, cr, wz, wr, ws, mc, mz, mr,
+    gp, gz, gs, gf, y, yr, ms_send, ms_recv,
     w1s, w1r, wss, wsr, w2s, w2r, m1s, m1r, m2s, m2r, g1s, g1r, g2s, g2r, c1s, c1r, c3s, c3r, xs, xr,
 ):
     rooms = 2 * n
@@ -64,15 +65,24 @@
     def greet_column(d):
         pl.semaphore_signal(barrier, inc=1, device_id=in_column(lax.rem(z + d, n)), device_id_type=MESH)
 
+    back = lax.rem(z - g + 2 * n + 1, 4) - 1
+    from_plane = lax.rem(z - back + n, n)
+
+    def greet_senders(q):
+        pl.semaphore_signal(barrier, inc=1, device_id=(q // 2, 2 * from_plane + lax.rem(q, 2)), device_id_type=MESH)
+
+    @pl.when(back != 0)
+    def _():
+        loop(0, rooms, greet_senders)
+
     loop(1, rooms, greet_plane)
     loop(1, n, greet_column)
-    pl.semaphore_wait(barrier, rooms - 1 + n - 1)
-
-    def w1_copy(q):
-        return remote(w_ref, wz.at[z], w1s.at[q], w1r.at[z], in_column(q))
-
-    def w1_arrival(q):
-        return remote(w_ref, wz.at[q], w1s.at[q], w1r.at[q], in_column(q))
+    pl.semaphore_wait(barrier, rooms - 1 + n - 1 + 3 * 4 * 2)
+
+    far = (n // 2, n // 4, 3 * n // 4)
+
+    def w1_copy(k):
+        return remote(w_ref, wz.at[k], w1s.at[k], w1r.at[k], in_column(lax.rem(z + far[k], n)))
 
     def ws_copy(q):
         return remote(w_ref, ws.at[g], wss.at[q], wsr.at[g], (q, f))
@@ -80,10 +90,53 @@
     def ws_arrival(q):
         return remote(w_ref, ws.at[q], wss.at[q], wsr.at[q], (q, f))
 
-    loop(1, n, lambda d: w1_copy(lax.rem(z + d, n)).start())
+    for k in range(3):
+        w1_copy(k).start()
+
+    near = (2, 1, n - 1, 0)
+
+    def w2_each(k, act):
+        src = w_ref if k == 3 else wz.at[k]
+        origin = z if k == 3 else lax.rem(z + n - far[k], n)
+        for e in range(4):
+            for side in range(2):
+                plane = lax.rem(z + near[e], n)
+                copy = remote(
+                    src, wr.at[g, h], w2s.at[8 * k + 2 * e + side], w2r.at[me], (origin, 2 * plane + side)
+                )
+                if e < 3:
+                    act(copy)
+                else:
+
+                    @pl.when((origin != g) | (h != side))
+                    def _():
+                        act(copy)
+
+    def w2_arrival(q):
+        return remote(w_ref, wr.at[q // 2, lax.rem(q, 2)], w2s.at[0], w2r.at[q], in_plane(q))
+
+    w2_each(3, lambda copy: copy.start())
     loop(1, n, lambda d: ws_copy(lax.rem(g + d, n)).start())
-    wz[z] = w_ref[...]
     ws[g] = w_ref[...]
+
+    clips = len_ref.shape[1]
+    row = lax.broadcasted_iota(jnp.int32, (rows, clips), 0)
+    other = lax.broadcasted_iota(jnp.int32, (rows, clips), 1)
+    lengths = jnp.broadcast_to(len_ref[...].astype(jnp.float32), (rows, clips))
+    routes = jnp.broadcast_to(route_ref[...].astype(jnp.float32), (rows, clips))
+
+    def total(kept, of):
+        return jnp.sum(jnp.where(kept, of, 0.0), axis=1, keepdims=True)
+
+    length = total(other == row // 8, lengths)
+    route = total(other == row // 8, routes)
+    rank = total((other < row // 8) & (routes == route), jnp.ones_like(routes))
+    frame = (lax.broadcasted_iota(jnp.int32, (rows, 1), 0) % 8).astype(jnp.float32)
+    slot = jnp.where(frame < length, (route * SLOTS + rank) * 8.0 + frame, -1.0)
+    slot_all = jnp.broadcast_to(slot, (rows, 128))
+    slot_col[...] = slot_all
+    slot_row[...] = jnp.transpose(slot_all)[:8, :]
+    weight[...] = jnp.broadcast_to(jnp.where(frame < length, 1.0 / length, 0.0), (rows, 128))
 
     wide = bins + 128
     coarse = window // 64
@@ -126,6 +179,19 @@
 
     loop(0, coarse, table_rows)
 
+    for k in range(3):
+        w1_copy(k).wait_recv()
+        w2_each(k, lambda copy: copy.start())
+
+    @pl.when(back == 0)
+    def _():
+        for k in range(4):
+            origin = z if k == 3 else lax.rem(z + n - far[k], n)
+
+            @pl.when(origin == g)
+            def _():
+                wr[g, h] = w_ref[...] if k == 3 else wz[k]
+
     block = min(256, bins)
 
     def spectra_block(i):
@@ -135,7 +201,7 @@
         re = jnp.dot(frames, tab[:, here], preferred_element_type=jnp.float32)
         im = jnp.dot(frames, tab[:, there], preferred_element_type=jnp.float32)
         energy = jnp.log1p((re * re + im * im) / window)
-        kept = (energy * live_ref[...]).reshape(rows // 8, 8, block)
+        kept = (energy * weight[:, :1]).reshape(rows // 8, 8, block)
         mean = jnp.sum(kept, axis=1, keepdims=True)
         centered = energy.reshape(rows // 8, 8, block) - mean
         c_own[:, here] = centered.reshape(rows, block).astype(jnp.bfloat16)
@@ -145,32 +211,10 @@
     pair_copy = remote(c_own, c_pair, xs.at[0], xr.at[0], pair)
     pair_copy.start()
 
-    def w2_copy(src, q):
-        return remote(wz.at[src], wr.at[g, h], w2s.at[q], w2r.at[me], in_plane(q))
-
-    def w2_arrival(q):
-        return remote(wz.at[0], wr.at[q // 2, lax.rem(q, 2)], w2s.at[q], w2r.at[q], in_plane(q))
-
-    def w2_send(src):
-        for side in range(2):
-            q = 2 * src + side
-
-            @pl.when(q != me)
-            def _():
-                w2_copy(src, q).start()
-
-    def w2_forward(d):
-        src = lax.rem(z + d, n)
-        w1_arrival(src).wait_recv()
-        w2_send(src)
-
-    w2_send(z)
-    loop(1, n, w2_forward)
-    wr[g, h] = wz[g]
-
     width = cs.shape[1]
     place = (
-        lax.broadcasted_iota(jnp.int32, (rooms * width, rows), 0) == srow_ref[...]
+        lax.broadcasted_iota(jnp.int32, (rooms * width, rows), 0).astype(jnp.float32)
+        == slot_row[:1, :]
     ).astype(jnp.bfloat16)
 
     def place_block(i):
@@ -189,7 +233,12 @@
     loop(1, rooms, lambda d: c1_copy(lax.rem(me + d, rooms)).start())
     cr[me] = cs[me]
 
-    loop(1, rooms, lambda d: w2_arrival(lax.rem(me + d, rooms)).wait_recv())
+    def w2_wait(q):
+        @pl.when((q != me) | (back != 0))
+        def _():
+            w2_arrival(q).wait_recv()
+
+    loop(0, rooms, w2_wait)
     loop(1, n, lambda d: ws_arrival(lax.rem(g + d, n)).wait_recv())
 
     w_rows = jnp.concatenate([wr[k].reshape(2 * rb, -1) for k in range(n)], axis=1)
@@ -215,17 +264,48 @@
     loop(1, n, lambda d: g1_copy(lax.rem(z + d, n)).start())
     gz[z] = gp[...]
 
-    scaled = (w_rows.astype(jnp.float32) * gain_ref[...]).astype(jnp.bfloat16)
-    mc[...] = jnp.dot(scaled, head_ref[...], preferred_element_type=jnp.float32).astype(jnp.bfloat16)
-
-    def m1_copy(q):
-        return remote(mc, mz.at[z], m1s.at[q], m1r.at[z], in_column(q))
-
-    def m1_arrival(q):
-        return remote(mc, mz.at[q], m1s.at[q], m1r.at[q], in_column(q))
-
-    loop(1, n, lambda d: m1_copy(lax.rem(z + d, n)).start())
-    mz[z] = mc[...]
+    scaled = w_rows.astype(jnp.float32) * gain_ref[...]
+    scaled_high = scaled.astype(jnp.bfloat16)
+    scaled_low = (scaled - scaled_high.astype(jnp.float32)).astype(jnp.bfloat16)
+    both = jnp.concatenate([scaled_high, scaled_low], axis=0)
+    product = jnp.dot(both, head_ref[...], preferred_element_type=jnp.float32)
+    mc[...] = (product[: 2 * rb] + product[2 * rb :]).astype(jnp.bfloat16)
+
+    def m1_copy(k):
+        return remote(mc, mz.at[k], m1s.at[k], m1r.at[k], in_column(lax.rem(z + far[k], n)))
+
+    def m2_each(k, act):
+        src = mc if k == 3 else mz.at[k]
+        origin = z if k == 3 else lax.rem(z + n - far[k], n)
+        for e in range(4):
+            plane = lax.rem(z + near[e], n)
+            copy = remote(src, mr.at[g], m2s.at[4 * k + e], m2r.at[g], (origin, 2 * plane + h))
+            if e < 3:
+                act(copy)
+            else:
+
+                @pl.when(origin != g)
+                def _():
+                    act(copy)
+
+    def m2_arrival(q):
+        return remote(mc, mr.at[q], m2s.at[0], m2r.at[q], (q, f))
+
+    for k in range(3):
+        m1_copy(k).start()
+    m2_each(3, lambda copy: copy.start())
+    for k in range(3):
+        m1_copy(k).wait_recv()
+        m2_each(k, lambda copy: copy.start())
+
+    @pl.when(back == 0)
+    def _():
+        for k in range(4):
+            origin = z if k == 3 else lax.rem(z + n - far[k], n)
+
+            @pl.when(origin == g)
+            def _():
+                mr[g] = mc[...] if k == 3 else mz[k]
 
     loop(1, n, lambda d: g1_arrival(lax.rem(z + d, n)).wait_recv())
     for tile in range(n // 4):
@@ -262,50 +342,13 @@
     def _():
         gf[g] = gs[...]
 
-    def m2_copy(q):
-        return remote(mz.at[q], mr.at[g], m2s.at[q], m2r.at[g], (q, f))
-
-    def m2_arrival(q):
-        return remote(mz.at[q], mr.at[q], m2s.at[q], m2r.at[q], (q, f))
-
-    def m2_send(src):
-        @pl.when(src != g)
+    loop(1, rooms, lambda d: c1_arrival(lax.rem(me + d, rooms)).wait_recv())
+    def m2_wait(q):
+        @pl.when((q != g) | (back != 0))
         def _():
-            m2_copy(src).start()
-
-    def m2_forward(d):
-        src = lax.rem(z + d, n)
-        m1_arrival(src).wait_recv()
-        m2_send(src)
-
-    m2_send(z)
-    loop(1, n, m2_forward)
-    mr[g] = mz[g]
-
-    pair_copy.wait_recv()
-
-    def g2_wait(k):
-        @pl.when((k != g) | (h != core))
-        def _():
-            g2_arrival(k).wait_recv()
-
-    loop(0, n, g2_wait)
-    mine = pl.ds(pl.multiple_of(core * half, half), half)
-    gram_low = gf[:, :rb, :].reshape(half, half)
-    gram_high = gf[:, rb:, :].reshape(half, half)
-
-    def squares(frames):
-        out = jnp.dot(frames[:, :half], gram_low, preferred_element_type=jnp.float32)
-        out = out + jnp.dot(frames[:, half:], gram_high, preferred_element_type=jnp.float32)
-        return jnp.sum(out * frames[:, mine].astype(jnp.float32), axis=1, keepdims=True)
-
-    ms_send[...] = jnp.broadcast_to(squares(c_pair), ms_send.shape)
-    ms_copy = remote(ms_send, ms_recv, xs.at[1], xr.at[1], pair)
-    ms_copy.start()
-    squares_here = squares(c_own)
-
-    loop(1, rooms, lambda d: c1_arrival(lax.rem(me + d, rooms)).wait_recv())
-    loop(1, n, lambda d: m2_arrival(lax.rem(g + d, n)).wait_recv())
+            m2_arrival(q).wait_recv()
+
+    loop(0, n, m2_wait)
     low = mr[:, :rb, :].reshape(half, -1)
     high = mr[:, rb:, :].reshape(half, -1)
     got = cr[...].reshape(rooms * width, bins)
@@ -322,26 +365,51 @@
     loop(1, rooms, lambda d: c3_copy(lax.rem(me + d, rooms)).start())
     yr[me] = y[me]
 
-    loop(1, n, lambda d: w1_copy(lax.rem(z + d, n)).wait_send())
+    pair_copy.wait_recv()
+
+    def g2_wait(k):
+        @pl.when((k != g) | (h != core))
+        def _():
+            g2_arrival(k).wait_recv()
+
+    loop(0, n, g2_wait)
+    mine = pl.ds(pl.multiple_of(core * half, half), half)
+    gram_low = gf[:, :rb, :].reshape(half, half)
+    gram_high = gf[:, rb:, :].reshape(half, half)
+
+    def squares(frames):
+        out = jnp.dot(frames[:, :half], gram_low, preferred_element_type=jnp.float32)
+        out = out + jnp.dot(frames[:, half:], gram_high, preferred_element_type=jnp.float32)
+        return jnp.sum(out * frames[:, mine].astype(jnp.float32), axis=1, keepdims=True)
+
+    ms_send[...] = jnp.broadcast_to(squares(c_pair), ms_send.shape)
+    ms_copy = remote(ms_send, ms_recv, xs.at[1], xr.at[1], pair)
+    ms_copy.start()
+    squares_here = squares(c_own)
+
+    for k in range(3):
+        w1_copy(k).wait_send()
+        m1_copy(k).wait_send()
+    for k in range(4):
+        w2_each(k, lambda copy: copy.wait_send())
+        m2_each(k, lambda copy: copy.wait_send())
     loop(1, n, lambda d: ws_copy(lax.rem(g + d, n)).wait_send())
     loop(1, n, lambda d: g1_copy(lax.rem(z + d, n)).wait_send())
-    loop(1, n, lambda d: m1_copy(lax.rem(z + d, n)).wait_send())
-    loop(1, n, lambda d: m2_copy(lax.rem(g + d, n)).wait_send())
-    loop(1, rooms, lambda d: w2_copy(0, lax.rem(me + d, rooms)).wait_send())
     loop(1, rooms, lambda d: c1_copy(lax.rem(me + d, rooms)).wait_send())
     loop(0, n, g2_each(lambda copy: copy.wait_send()))
     pair_copy.wait_send()
 
     ms_copy.wait()
-    total = squares_here + ms_recv[:, :1]
-    mean_square = jnp.maximum(total, 0.0) / head_ref.shape[0]
+    square_sum = squares_here + ms_recv[:, :1]
+    mean_square = jnp.maximum(square_sum, 0.0) / head_ref.shape[0]
     scale = lax.rsqrt(mean_square + norm_epsilon)
     take = (
-        lax.broadcasted_iota(jnp.int32, (rows, rooms * width), 1) == scol_ref[...]
+        lax.broadcasted_iota(jnp.int32, (rows, rooms * width), 1).astype(jnp.float32)
+        == slot_col[:, :1]
     ).astype(jnp.bfloat16)
     loop(1, rooms, lambda d: c3_arrival(lax.rem(me + d, rooms)).wait_recv())
-    back = jnp.dot(take, yr[...].reshape(rooms * width, -1), preferred_element_type=jnp.float32)
-    out_ref[...] = (back * scale).astype(jnp.bfloat16)
+    found = jnp.dot(take, yr[...].reshape(rooms * width, -1), preferred_element_type=jnp.float32)
+    out_ref[...] = (found * scale).astype(jnp.bfloat16)
     loop(1, rooms, lambda d: c3_copy(lax.rem(me + d, rooms)).wait_send())
 
 
@@ -355,37 +423,30 @@
     curve = room_heads.shape[2]
     width = SLOTS * slots
 
-    lengths = clip_lengths.reshape(clip_count)
-    target = clip_routes.reshape(clip_count)
-    clip_idx = jnp.arange(clip_count, dtype=jnp.int32)
-    frame_idx = jnp.arange(slots, dtype=jnp.int32)
-    same = (target[:, None] == target[None, :]) & (clip_idx[:, None] > clip_idx[None, :])
-    slot = target * SLOTS + jnp.sum(same.astype(jnp.int32), axis=1)
-    live = frame_idx[None, :] < lengths[:, None]
-    slot_rows = jnp.where(live, slot[:, None] * slots + frame_idx[None, :], -1)
-    weights = live.astype(jnp.float32) / lengths[:, None].astype(jnp.float32)
-
     bf16, f32 = jnp.bfloat16, jnp.float32
     vmem, sems = pltpu.VMEM, lambda k: pltpu.SemaphoreType.DMA((k,))
     coarse = window // 64
     out = pl.pallas_call(
         functools.partial(kernel, n),
         out_shape=jax.ShapeDtypeStruct((rows, curve), bf16),
-        in_specs=[pl.BlockSpec(memory_space=pltpu.VMEM)] * 7,
+        in_specs=[pl.BlockSpec(memory_space=pltpu.VMEM)] * 6,
         out_specs=pl.BlockSpec(memory_space=pltpu.VMEM),
         scratch_shapes=[
             vmem((window, 2 * bins), bf16),
             vmem((coarse + 16, bins + 128), f32),
             vmem((coarse + 16, bins + 128), f32),
+            vmem((rows, 128), f32),
+            vmem((8, rows), f32),
+            vmem((rows, 128), f32),
             vmem((rows, bins), bf16),
             vmem((rows, bins), bf16),
             vmem((rooms, width, bins), bf16),
             vmem((rooms, width, bins), bf16),
-            vmem((n, rb, kc), bf16),
+            vmem((3, rb, kc), bf16),
             vmem((n, 2, rb, kc), bf16),
             vmem((n, rb, kc), bf16),
             vmem((2 * rb, curve), bf16),
-            vmem((n, 2 * rb, curve), bf16),
+            vmem((3, 2 * rb, curve), bf16),
             vmem((n, 2 * rb, curve), bf16),
             vmem((16, 128), bf16),
             vmem((n, 16, 128), bf16),
@@ -395,9 +456,9 @@
             vmem((rooms, width, curve), bf16),
             vmem((rows, 128), f32),
             vmem((rows, 128), f32),
-            sems(n), sems(n), sems(n), sems(n),
+            sems(3), sems(3), sems(n), sems(n),
             sems(rooms), sems(rooms),
-            sems(n), sems(n), sems(n), sems(n),
+            sems(3), sems(3), sems(16), sems(n),
             sems(n), sems(n), sems(n), sems(n),
             sems(rooms), sems(rooms), sems(rooms), sems(rooms),
             sems(2), sems(2),
@@ -410,9 +471,8 @@
         w_spectral,
         norm_gain.reshape(1, -1),
         room_heads[0],
-        slot_rows.reshape(1, rows),
-        slot_rows.reshape(rows, 1),
-        weights.reshape(rows, 1),
+        clip_lengths.reshape(1, clip_count),
+        clip_routes.reshape(1, clip_count),
     )
     return out.reshape(1, clip_count, slots, curve)
 

time: 103 us -> 76.7 us (0.74)
  the two profiles are of different devices: /device:TPU:1 before, /device:TPU:2 now
where the time goes in v2:
time: 76.7 us; the launch traced here: 76.5 us
  Pallas kernels  74.9 us (98%)
  local copies, waits for them, and re-layouts  1.57 us (2%)
    pallas_call x1, Pallas kernels, body(): pl.pallas_call(functools.partial(kernel, n), out_shape=jax.ShapeDtypeStru...  74.9 us
    unnamed x1, local copies, waits for them, and re-layouts  1.57 us

profile of v2, /device:TPU:2, one launch (start us, length us, event | category | flops | bytes accessed | tf_op | source)
XLA Modules:
  0.0 76.5 jit_solution(2490511975571067999)
XLA Ops:
  0.0 74.9 %shard_map.64 = bf16[256,256]{1,0:T(8,128)(2,1)} custom-call(bf16[256,2048]{1,0:T(8,128)(2,1)} %bitcast.7, bf16[32,256]{1,0:T(8,128)(2,1)} %w_ref.1, f32[1,4096]{1,0:T(1,128)} %bitcast.9, bf16[4096,256]{1,0:T(8,128)(2,1)} %bitcast.6, s32[1,32]{1,0:T(1,128)} %bitcast.10, s32[1,32]{1,0:T(1,128)} %bitcast.11), custom_call_target="tpu_custom_call" | custom-call | tf_op jit(solution)/shard_map/pallas_call | solution.py:429
  75.0 1.6 %copy.8 = bf16[1,32,8,256]{3,2,1,0:T(8,128)(2,1)} copy(bf16[1,32,8,256]{3,2,1,0:T(8,128)(2,1)} %bitcast.8) | data formatting | bytes 262144

commit v3 on v2

--- a/solution.py
+++ b/solution.py
@@ -34,10 +34,11 @@
 
 def kernel(
     n,
-    raw_ref, w_ref, gain_ref, head_ref, len_ref, route_ref,
+    raw_hbm, w_hbm, gain_hbm, head_hbm, len_hbm, route_hbm,
     out_ref,
+    raw_ref, w_ref, gain_ref, head_ref, len_ref, route_ref, loads,
     tab, trc, trs, slot_col, slot_row, weight, c_own, c_pair, cs, cr, wz, wr, ws, mc, mz, mr,
-    gp, gz, gs, gf, y, yr, ms_send, ms_recv,
+    gp, gz, gs, gf, y, yr, ms_send, ms_own, ms_recv,
     w1s, w1r, wss, wsr, w2s, w2r, m1s, m1r, m2s, m2r, g1s, g1r, g2s, g2r, c1s, c1r, c3s, c3r, xs, xr,
 ):
     rooms = 2 * n
@@ -58,6 +59,9 @@
         return (g, 2 * q + h)
 
     barrier = pltpu.get_barrier_semaphore()
+    placed = ((w_hbm, w_ref), (len_hbm, len_ref), (route_hbm, route_ref), (raw_hbm, raw_ref), (head_hbm, head_ref), (gain_hbm, gain_ref))
+    load = [pltpu.make_async_copy(src, dst, loads.at[k]) for k, (src, dst) in enumerate(placed)]
+    load[0].start()
 
     def greet_plane(d):
         pl.semaphore_signal(barrier, inc=1, device_id=in_plane(lax.rem(me + d, rooms)), device_id_type=MESH)
@@ -66,7 +70,7 @@
         pl.semaphore_signal(barrier, inc=1, device_id=in_column(lax.rem(z + d, n)), device_id_type=MESH)
 
     back = lax.rem(z - g + 2 * n + 1, 4) - 1
-    from_plane = lax.rem(z - back + n, n)
+    from_plane = lax.rem(z - back + 4 * lax.rem(g, 2) * ((back + 1) // 3) + n, n)
 
     def greet_senders(q):
         pl.semaphore_signal(barrier, inc=1, device_id=(q // 2, 2 * from_plane + lax.rem(q, 2)), device_id_type=MESH)
@@ -77,6 +81,9 @@
 
     loop(1, rooms, greet_plane)
     loop(1, n, greet_column)
+    for copy in load[1:]:
+        copy.start()
+    load[0].wait()
     pl.semaphore_wait(barrier, rooms - 1 + n - 1 + 3 * 4 * 2)
 
     far = (n // 2, n // 4, 3 * n // 4)
@@ -93,7 +100,7 @@
     for k in range(3):
         w1_copy(k).start()
 
-    near = (2, 1, n - 1, 0)
+    near = (n + 2 - 4 * lax.rem(z, 2), 1, n - 1, 0)
 
     def w2_each(k, act):
         src = w_ref if k == 3 else wz.at[k]
@@ -118,6 +125,9 @@
     w2_each(3, lambda copy: copy.start())
     loop(1, n, lambda d: ws_copy(lax.rem(g + d, n)).start())
     ws[g] = w_ref[...]
+
+    load[1].wait()
+    load[2].wait()
 
     clips = len_ref.shape[1]
     row = lax.broadcasted_iota(jnp.int32, (rows, clips), 0)
@@ -206,6 +216,7 @@
         centered = energy.reshape(rows // 8, 8, block) - mean
         c_own[:, here] = centered.reshape(rows, block).astype(jnp.bfloat16)
 
+    load[3].wait()
     loop(0, bins // block, spectra_block)
 
     pair_copy = remote(c_own, c_pair, xs.at[0], xr.at[0], pair)
@@ -225,11 +236,10 @@
     loop(0, bins // block, place_block)
 
     def c1_copy(q):
-        return remote(cs.at[q], cr.at[me], c1s.at[q], c1r.at[me], in_plane(q))
-
-    def c1_arrival(q):
-        return remote(cs.at[q], cr.at[q], c1s.at[q], c1r.at[q], in_plane(q))
-
+        return remote(cs.at[q], cr.at[me], c1s.at[0], c1r.at[0], in_plane(q))
+
+    others = pl.ds(0, rooms - 1)
+    c1_all = remote(cs.at[others], cr.at[others], c1s.at[0], c1r.at[0], pair)
     loop(1, rooms, lambda d: c1_copy(lax.rem(me + d, rooms)).start())
     cr[me] = cs[me]
 
@@ -242,6 +252,38 @@
     loop(1, n, lambda d: ws_arrival(lax.rem(g + d, n)).wait_recv())
 
     w_rows = jnp.concatenate([wr[k].reshape(2 * rb, -1) for k in range(n)], axis=1)
+    load[4].wait()
+    load[5].wait()
+    scaled = w_rows.astype(jnp.float32) * gain_ref[...]
+    scaled_high = scaled.astype(jnp.bfloat16)
+    scaled_low = (scaled - scaled_high.astype(jnp.float32)).astype(jnp.bfloat16)
+    both = jnp.concatenate([scaled_high, scaled_low], axis=0)
+    product = jnp.dot(both, head_ref[...], preferred_element_type=jnp.float32)
+    mc[...] = (product[: 2 * rb] + product[2 * rb :]).astype(jnp.bfloat16)
+
+    def m1_copy(k):
+        return remote(mc, mz.at[k], m1s.at[k], m1r.at[k], in_column(lax.rem(z + far[k], n)))
+
+    def m2_each(k, act):
+        src = mc if k == 3 else mz.at[k]
+        origin = z if k == 3 else lax.rem(z + n - far[k], n)
+        for e in range(4):
+            plane = lax.rem(z + near[e], n)
+            copy = remote(src, mr.at[g], m2s.at[4 * k + e], m2r.at[g], (origin, 2 * plane + h))
+            if e < 3:
+                act(copy)
+            else:
+
+                @pl.when(origin != g)
+                def _():
+                    act(copy)
+
+    def m2_arrival(q):
+        return remote(mc, mr.at[q], m2s.at[0], m2r.at[q], (q, f))
+
+    for k in range(3):
+        m1_copy(k).start()
+    m2_each(3, lambda copy: copy.start())
     w_cols = jnp.concatenate([ws[k] for k in range(n)], axis=1)
     gram = lax.dot_general(
         w_rows,
@@ -253,47 +295,21 @@
     piece = jnp.zeros((16, 128), jnp.float32)
     for q in range(4):
         piece = jnp.where(quarter == q, gram[16 * q : 16 * q + 16, :], piece)
-    gp[...] = piece.astype(jnp.bfloat16)
+    shift = lax.rem(z - g + n, n)
+    twice = jnp.where((shift > 0) & (shift < n // 2), 2.0, 1.0)
+    gp[...] = (piece * twice).astype(jnp.bfloat16)
 
     def g1_copy(q):
-        return remote(gp, gz.at[z], g1s.at[q], g1r.at[z], in_column(q))
-
-    def g1_arrival(q):
-        return remote(gp, gz.at[q], g1s.at[q], g1r.at[q], in_column(q))
-
-    loop(1, n, lambda d: g1_copy(lax.rem(z + d, n)).start())
-    gz[z] = gp[...]
-
-    scaled = w_rows.astype(jnp.float32) * gain_ref[...]
-    scaled_high = scaled.astype(jnp.bfloat16)
-    scaled_low = (scaled - scaled_high.astype(jnp.float32)).astype(jnp.bfloat16)
-    both = jnp.concatenate([scaled_high, scaled_low], axis=0)
-    product = jnp.dot(both, head_ref[...], preferred_element_type=jnp.float32)
-    mc[...] = (product[: 2 * rb] + product[2 * rb :]).astype(jnp.bfloat16)
-
-    def m1_copy(k):
-        return remote(mc, mz.at[k], m1s.at[k], m1r.at[k], in_column(lax.rem(z + far[k], n)))
-
-    def m2_each(k, act):
-        src = mc if k == 3 else mz.at[k]
-        origin = z if k == 3 else lax.rem(z + n - far[k], n)
-        for e in range(4):
-            plane = lax.rem(z + near[e], n)
-            copy = remote(src, mr.at[g], m2s.at[4 * k + e], m2r.at[g], (origin, 2 * plane + h))
-            if e < 3:
-                act(copy)
-            else:
-
-                @pl.when(origin != g)
-                def _():
-                    act(copy)
-
-    def m2_arrival(q):
-        return remote(mc, mr.at[q], m2s.at[0], m2r.at[q], (q, f))
-
-    for k in range(3):
-        m1_copy(k).start()
-    m2_each(3, lambda copy: copy.start())
+        return remote(gp, gz.at[shift], g1s.at[q], g1r.at[shift], in_column(q))
+
+    def g1_arrival(k):
+        return remote(gp, gz.at[k], g1s.at[0], g1r.at[k], in_column(lax.rem(g + k, n)))
+
+    @pl.when(shift <= n // 2)
+    def _():
+        loop(1, n, lambda d: g1_copy(lax.rem(z + d, n)).start())
+        gz[shift] = gp[...]
+
     for k in range(3):
         m1_copy(k).wait_recv()
         m2_each(k, lambda copy: copy.start())
@@ -307,22 +323,18 @@
             def _():
                 mr[g] = mc[...] if k == 3 else mz[k]
 
-    loop(1, n, lambda d: g1_arrival(lax.rem(z + d, n)).wait_recv())
-    for tile in range(n // 4):
-        pieces = [gz[4 * tile + k].astype(jnp.float32) for k in range(4)]
-        for q in range(4):
-            strip = jnp.zeros((16, 128), jnp.float32)
-            for k in range(4):
-                shift = (rb * (k - q)) % 128
-                moved = pltpu.roll(pieces[k], shift, 1) if shift else pieces[k]
-                strip = jnp.where(quarter == k, moved, strip)
-            gs[16 * q : 16 * q + 16, 128 * tile : 128 * tile + 128] = strip.astype(jnp.bfloat16)
+    def g1_wait(k):
+        @pl.when(k != shift)
+        def _():
+            g1_arrival(k).wait_recv()
+
+    loop(0, n // 2 + 1, g1_wait)
 
     def g2_copy(q):
-        return remote(gs, gf.at[g], g2s.at[q], g2r.at[g], (2 * (q // 2) + h, 2 * z + lax.rem(q, 2)))
+        return remote(gz, gf.at[g], g2s.at[q], g2r.at[g], (2 * (q // 2) + h, 2 * z + lax.rem(q, 2)))
 
     def g2_arrival(k):
-        return remote(gs, gf.at[k], g2s.at[0], g2r.at[k], (k, 2 * z + core))
+        return remote(gz, gf.at[k], g2s.at[0], g2r.at[k], (k, 2 * z + core))
 
     own = 2 * (g // 2) + h
 
@@ -340,9 +352,9 @@
 
     @pl.when(h == core)
     def _():
-        gf[g] = gs[...]
-
-    loop(1, rooms, lambda d: c1_arrival(lax.rem(me + d, rooms)).wait_recv())
+        gf[g] = gz[...]
+
+    c1_all.wait_recv()
     def m2_wait(q):
         @pl.when((q != g) | (back != 0))
         def _():
@@ -357,11 +369,9 @@
     y[...] = curves.astype(jnp.bfloat16).reshape(y.shape)
 
     def c3_copy(q):
-        return remote(y.at[q], yr.at[me], c3s.at[q], c3r.at[me], in_plane(q))
-
-    def c3_arrival(q):
-        return remote(y.at[q], yr.at[q], c3s.at[q], c3r.at[q], in_plane(q))
-
+        return remote(y.at[q], yr.at[me], c3s.at[0], c3r.at[0], in_plane(q))
+
+    c3_all = remote(y.at[others], yr.at[others], c3s.at[0], c3r.at[0], pair)
     loop(1, rooms, lambda d: c3_copy(lax.rem(me + d, rooms)).start())
     yr[me] = y[me]
 
@@ -373,19 +383,34 @@
             g2_arrival(k).wait_recv()
 
     loop(0, n, g2_wait)
-    mine = pl.ds(pl.multiple_of(core * half, half), half)
-    gram_low = gf[:, :rb, :].reshape(half, half)
-    gram_high = gf[:, rb:, :].reshape(half, half)
-
-    def squares(frames):
-        out = jnp.dot(frames[:, :half], gram_low, preferred_element_type=jnp.float32)
-        out = out + jnp.dot(frames[:, half:], gram_high, preferred_element_type=jnp.float32)
-        return jnp.sum(out * frames[:, mine].astype(jnp.float32), axis=1, keepdims=True)
-
-    ms_send[...] = jnp.broadcast_to(squares(c_pair), ms_send.shape)
+    def squares_of_group(m):
+        for r in range(4):
+            for q in range(4):
+                pieces = [gf[4 * m + r, k].astype(jnp.float32) for k in range(n // 2 + 1)]
+                for tile in range(3):
+                    strip = jnp.zeros((16, 128), jnp.float32)
+                    for k in range(4):
+                        s = 4 * tile + k - r
+                        if 0 <= s <= n // 2:
+                            turn = (rb * (k - q)) % 128
+                            moved = pltpu.roll(pieces[s], turn, 1) if turn else pieces[s]
+                            strip = jnp.where(quarter == k, moved, strip)
+                    low = 128 * (q // 2) + rb * r + 16 * (q % 2)
+                    gs[low : low + 16, 128 * tile : 128 * tile + 128] = strip.astype(jnp.bfloat16)
+        wide_low = pl.ds(pl.multiple_of(128 * m, 128), 128)
+        wide_high = pl.ds(pl.multiple_of(half + 128 * m, 128), 128)
+        for frames, sums in ((c_pair, ms_send), (c_own, ms_own)):
+            part = jnp.concatenate([frames[:, wide_low], frames[:, wide_high]], axis=1)
+            out = jnp.dot(part, gs[...], preferred_element_type=jnp.float32)
+            for tile in range(3):
+                cols = pl.ds(pl.multiple_of(core * half + 128 * lax.rem(m + tile, n // 4), 128), 128)
+                sums[...] += out[:, 128 * tile : 128 * tile + 128] * frames[:, cols].astype(jnp.float32)
+
+    ms_send[...] = jnp.zeros_like(ms_send)
+    ms_own[...] = jnp.zeros_like(ms_own)
+    loop(0, n // 4, squares_of_group)
     ms_copy = remote(ms_send, ms_recv, xs.at[1], xr.at[1], pair)
     ms_copy.start()
-    squares_here = squares(c_own)
 
     for k in range(3):
         w1_copy(k).wait_send()
@@ -394,23 +419,27 @@
         w2_each(k, lambda copy: copy.wait_send())
         m2_each(k, lambda copy: copy.wait_send())
     loop(1, n, lambda d: ws_copy(lax.rem(g + d, n)).wait_send())
-    loop(1, n, lambda d: g1_copy(lax.rem(z + d, n)).wait_send())
-    loop(1, rooms, lambda d: c1_copy(lax.rem(me + d, rooms)).wait_send())
+
+    @pl.when(shift <= n // 2)
+    def _():
+        loop(1, n, lambda d: g1_copy(lax.rem(z + d, n)).wait_send())
+
+    c1_all.wait_send()
     loop(0, n, g2_each(lambda copy: copy.wait_send()))
     pair_copy.wait_send()
 
     ms_copy.wait()
-    square_sum = squares_here + ms_recv[:, :1]
+    square_sum = jnp.sum(ms_own[...] + ms_recv[...], axis=1, keepdims=True)
     mean_square = jnp.maximum(square_sum, 0.0) / head_ref.shape[0]
     scale = lax.rsqrt(mean_square + norm_epsilon)
     take = (
         lax.broadcasted_iota(jnp.int32, (rows, rooms * width), 1).astype(jnp.float32)
         == slot_col[:, :1]
     ).astype(jnp.bfloat16)
-    loop(1, rooms, lambda d: c3_arrival(lax.rem(me + d, rooms)).wait_recv())
+    c3_all.wait_recv()
     found = jnp.dot(take, yr[...].reshape(rooms * width, -1), preferred_element_type=jnp.float32)
     out_ref[...] = (found * scale).astype(jnp.bfloat16)
-    loop(1, rooms, lambda d: c3_copy(lax.rem(me + d, rooms)).wait_send())
+    c3_all.wait_send()
 
 
 def body(raw_clips, clip_lengths, clip_routes, w_spectral, norm_gain, room_heads):
@@ -426,12 +455,27 @@
     bf16, f32 = jnp.bfloat16, jnp.float32
     vmem, sems = pltpu.VMEM, lambda k: pltpu.SemaphoreType.DMA((k,))
     coarse = window // 64
+    operands = (
+        raw_clips.reshape(rows, window),
+        w_spectral,
+        norm_gain.reshape(1, -1),
+        room_heads[0],
+        clip_lengths.reshape(1, clip_count),
+        clip_routes.reshape(1, clip_count),
+    )
     out = pl.pallas_call(
         functools.partial(kernel, n),
         out_shape=jax.ShapeDtypeStruct((rows, curve), bf16),
-        in_specs=[pl.BlockSpec(memory_space=pltpu.VMEM)] * 6,
+        in_specs=[pl.BlockSpec(memory_space=pltpu.HBM)] * 6,
         out_specs=pl.BlockSpec(memory_space=pltpu.VMEM),
         scratch_shapes=[
+            vmem((rows, window), bf16),
+            vmem((rb, kc), bf16),
+            vmem((1, n * kc), f32),
+            vmem((n * kc, curve), bf16),
+            vmem((1, clip_count), jnp.int32),
+            vmem((1, clip_count), jnp.int32),
+            sems(6),
             vmem((window, 2 * bins), bf16),
             vmem((coarse + 16, bins + 128), f32),
             vmem((coarse + 16, bins + 128), f32),
@@ -449,30 +493,26 @@
             vmem((3, 2 * rb, curve), bf16),
             vmem((n, 2 * rb, curve), bf16),
             vmem((16, 128), bf16),
-            vmem((n, 16, 128), bf16),
-            vmem((2 * rb, bins // 2), bf16),
-            vmem((n, 2 * rb, bins // 2), bf16),
+            vmem((n // 2 + 1, 16, 128), bf16),
+            vmem((256, 384), bf16),
+            vmem((n, n // 2 + 1, 16, 128), bf16),
             vmem((rooms, width, curve), bf16),
             vmem((rooms, width, curve), bf16),
+            vmem((rows, 128), f32),
             vmem((rows, 128), f32),
             vmem((rows, 128), f32),
             sems(3), sems(3), sems(n), sems(n),
             sems(rooms), sems(rooms),
             sems(3), sems(3), sems(16), sems(n),
             sems(n), sems(n), sems(n), sems(n),
-            sems(rooms), sems(rooms), sems(rooms), sems(rooms),
+            sems(1), sems(1), sems(1), sems(1),
             sems(2), sems(2),
         ],
         compiler_params=pltpu.CompilerParams(
-            collective_id=0, has_side_effects=True, vmem_limit_bytes=56 * 2**20
+            collective_id=0, has_side_effects=True, vmem_limit_bytes=32 * 2**20
         ),
     )(
-        raw_clips.reshape(rows, window),
-        w_spectral,
-        norm_gain.reshape(1, -1),
-        room_heads[0],
-        clip_lengths.reshape(1, clip_count),
-        clip_routes.reshape(1, clip_count),
+        *(pltpu.with_memory_space_constraint(x, pltpu.HBM) for x in operands)
     )
     return out.reshape(1, clip_count, slots, curve)
 

time: 76.7 us -> 65.8 us (0.86)
  the two profiles are of different devices: /device:TPU:2 before, /device:TPU:1 now
where the time goes in v3:
time: 65.8 us; the launch traced here: 65.7 us
  Pallas kernels  65 us (99%)
  local copies, waits for them, and re-layouts  0.66 us (1%)
    pallas_call x1, Pallas kernels, body(): pl.pallas_call(functools.partial(kernel, n), out_shape=jax.ShapeDtypeStru...  65 us

profile of v3, /device:TPU:1, one launch (start us, length us, event | category | flops | bytes accessed | tf_op | source)
XLA Modules:
  0.0 65.7 jit_solution(15462127197321020504)
XLA Ops:
  0.0 65.0 %shard_map.64 = bf16[256,256]{1,0:T(8,128)(2,1)S(1)} custom-call(bf16[256,2048]{1,0:T(8,128)(2,1)} %bitcast.8, bf16[32,256]{1,0:T(8,128)(2,1)} %w_hbm.1, f32[1,4096]{1,0:T(1,128)} %bitcast.9, bf16[4096,256]{1,0:T(8,128)(2,1)} %bitcast.7, s32[1,32]{1,0:T(1,128)} %bitcast.10, s32[1,32]{1,0:T(1,128)} %bitcast.11), custom_call_target="tpu_custom_call" | custom-call | tf_op jit(solution)/shard_map/pallas_call | solution.py:466
  65.0 0.7 %copy.8 = bf16[1,32,8,256]{3,2,1,0:T(8,128)(2,1)} copy(bf16[1,32,8,256]{3,2,1,0:T(8,128)(2,1)S(1)} %bitcast.6) | data formatting | bytes 262144

commit v4 on v3

--- a/solution.py
+++ b/solution.py
@@ -75,12 +75,13 @@
     def greet_senders(q):
         pl.semaphore_signal(barrier, inc=1, device_id=(q // 2, 2 * from_plane + lax.rem(q, 2)), device_id_type=MESH)
 
+    loop(1, n, greet_column)
+
     @pl.when(back != 0)
     def _():
         loop(0, rooms, greet_senders)
 
     loop(1, rooms, greet_plane)
-    loop(1, n, greet_column)
     for copy in load[1:]:
         copy.start()
     load[0].wait()
@@ -382,8 +383,8 @@
         def _():
             g2_arrival(k).wait_recv()
 
-    loop(0, n, g2_wait)
     def squares_of_group(m):
+        loop(4 * m, 4 * m + 4, g2_wait)
         for r in range(4):
             for q in range(4):
                 pieces = [gf[4 * m + r, k].astype(jnp.float32) for k in range(n // 2 + 1)]

time: 65.8 us -> 64 us (0.973)
  Pallas kernels: 65 us -> 63.1 us
    pallas_call x1, Pallas kernels: 65 us -> 63.1 us  [body(): pl.pallas_call(functools.partial(kernel, n), out_shape=jax.ShapeDtypeStru...]
where the time goes in v4:
time: 64 us; the launch traced here: 63.8 us
  Pallas kernels  63.1 us (99%)
  local copies, waits for them, and re-layouts  0.66 us (1%)
    pallas_call x1, Pallas kernels, body(): pl.pallas_call(functools.partial(kernel, n), out_shape=jax.ShapeDtypeStru...  63.1 us

profile of v4, /device:TPU:1, one launch (start us, length us, event | category | flops | bytes accessed | tf_op | source)
XLA Modules:
  0.0 63.8 jit_solution(3208456383336255085)
XLA Ops:
  0.0 63.1 %shard_map.64 = bf16[256,256]{1,0:T(8,128)(2,1)S(1)} custom-call(bf16[256,2048]{1,0:T(8,128)(2,1)} %bitcast.8, bf16[32,256]{1,0:T(8,128)(2,1)} %w_hbm.1, f32[1,4096]{1,0:T(1,128)} %bitcast.9, bf16[4096,256]{1,0:T(8,128)(2,1)} %bitcast.7, s32[1,32]{1,0:T(1,128)} %bitcast.10, s32[1,32]{1,0:T(1,128)} %bitcast.11), custom_call_target="tpu_custom_call" | custom-call | tf_op jit(solution)/shard_map/pallas_call | solution.py:467
  63.1 0.7 %copy.8 = bf16[1,32,8,256]{3,2,1,0:T(8,128)(2,1)} copy(bf16[1,32,8,256]{3,2,1,0:T(8,128)(2,1)S(1)} %bitcast.6) | data formatting | bytes 262144

commit v5 on v4

--- a/solution.py
+++ b/solution.py
@@ -75,7 +75,8 @@
     def greet_senders(q):
         pl.semaphore_signal(barrier, inc=1, device_id=(q // 2, 2 * from_plane + lax.rem(q, 2)), device_id_type=MESH)
 
-    loop(1, n, greet_column)
+    greet_column(n // 2)
+    loop(1, n // 2, lambda d: (greet_column(n // 2 - d), greet_column(n // 2 + d)))
 
     @pl.when(back != 0)
     def _():
@@ -341,7 +342,7 @@
 
     def g2_each(act):
         def step(d):
-            q = lax.rem(own + d, n)
+            q = lax.rem(own + n // 2 + d, n)
 
             @pl.when((2 * (q // 2) + h != g) | (lax.rem(q, 2) != h))
             def _():

time: 64 us -> 64 us (level)
  no operation moved by 1% of the time
where the time goes in v5:
time: 64 us; the launch traced here: 63.9 us
  Pallas kernels  63.2 us (99%)
  local copies, waits for them, and re-layouts  0.66 us (1%)
    pallas_call x1, Pallas kernels, body(): pl.pallas_call(functools.partial(kernel, n), out_shape=jax.ShapeDtypeStru...  63.2 us

profile of v5, /device:TPU:1, one launch (start us, length us, event | category | flops | bytes accessed | tf_op | source)
XLA Modules:
  0.0 63.9 jit_solution(4163046948565482173)
XLA Ops:
  0.0 63.2 %shard_map.64 = bf16[256,256]{1,0:T(8,128)(2,1)S(1)} custom-call(bf16[256,2048]{1,0:T(8,128)(2,1)} %bitcast.8, bf16[32,256]{1,0:T(8,128)(2,1)} %w_hbm.1, f32[1,4096]{1,0:T(1,128)} %bitcast.9, bf16[4096,256]{1,0:T(8,128)(2,1)} %bitcast.7, s32[1,32]{1,0:T(1,128)} %bitcast.10, s32[1,32]{1,0:T(1,128)} %bitcast.11), custom_call_target="tpu_custom_call" | custom-call | tf_op jit(solution)/shard_map/pallas_call | solution.py:468
  63.2 0.7 %copy.8 = bf16[1,32,8,256]{3,2,1,0:T(8,128)(2,1)} copy(bf16[1,32,8,256]{3,2,1,0:T(8,128)(2,1)S(1)} %bitcast.6) | data formatting | bytes 262144
